TPU v7x, 32 devices: a whole 2x2x4 slice. The times are simulated.
32 devices in a mesh: dp: 16 (over z, y, core), cp: 2 (over x).
Axes of the slice: x: 2, y: 2, z: 4, core: 2. Of those that a mesh axis runs over, the one named last changes fastest.
Arguments:
- tokens: bfloat16 [4096, 768], P(('dp', 'cp')), may hold values from -6 to 6
- segment_ids: int32 [4096], P(('dp', 'cp')), may hold values from 0 to 2, as said below
- cotangent: bfloat16 [4096, 768], P(('dp', 'cp')), may hold values from -6 to 6
- qkv_weight: bfloat16 [2, 768, 2304], P(None, ('dp', 'cp')), may hold values from -0.21875 to 0.21875
- qkv_bias: bfloat16 [2, 2304], P(None, ('dp', 'cp')), may hold values from -3 to 3
- attn_weight: bfloat16 [2, 768, 768], P(None, ('dp', 'cp')), may hold values from -1.75 to 1.75
- attn_bias: bfloat16 [2, 768], P(None, ('dp', 'cp')), may hold values from -2 to 2
- up_weight: bfloat16 [2, 768, 3072], P(None, ('dp', 'cp')), may hold values from -0.21875 to 0.21875
- up_bias: bfloat16 [2, 3072], P(None, ('dp', 'cp')), may hold values from -3 to 3
- down_weight: bfloat16 [2, 3072, 768], P(None, ('dp', 'cp')), may hold values from -0.109375 to 0.109375
- down_bias: bfloat16 [2, 768], P(None, ('dp', 'cp')), may hold values from -2 to 2
- attn_gain: bfloat16 [2, 768], P(None, ('dp', 'cp')), may hold values from 0.5 to 1.5
- attn_shift: bfloat16 [2, 768], P(None, ('dp', 'cp')), may hold values from -2 to 2
- mlp_gain: bfloat16 [2, 768], P(None, ('dp', 'cp')), may hold values from 0.5 to 1.5
- mlp_shift: bfloat16 [2, 768], P(None, ('dp', 'cp')), may hold values from -2 to 2
Outputs:
- activations: bfloat16 [4096, 768], P(('dp', 'cp'))
- input_grad: float32 [4096, 768], P(('dp', 'cp'))
- qkv_weight_grad: float32 [2, 768, 2304], P(None, ('dp', 'cp'))
- qkv_bias_grad: float32 [2, 2304], P(None, ('dp', 'cp'))
- attn_weight_grad: float32 [2, 768, 768], P(None, ('dp', 'cp'))
- attn_bias_grad: float32 [2, 768], P(None, ('dp', 'cp'))
- up_weight_grad: float32 [2, 768, 3072], P(None, ('dp', 'cp'))
- up_bias_grad: float32 [2, 3072], P(None, ('dp', 'cp'))
- down_weight_grad: float32 [2, 3072, 768], P(None, ('dp', 'cp'))
- down_bias_grad: float32 [2, 768], P(None, ('dp', 'cp'))
- attn_gain_grad: float32 [2, 768], P(None, ('dp', 'cp'))
- attn_shift_grad: float32 [2, 768], P(None, ('dp', 'cp'))
- mlp_gain_grad: float32 [2, 768], P(None, ('dp', 'cp'))
- mlp_shift_grad: float32 [2, 768], P(None, ('dp', 'cp'))
Inputs may be any that keep to these rules, and one draw needn't show every extreme that they name: `segment_ids`: within each group of 256 consecutive tokens the ids never fall; ids 0, 1 and 2 all occur, and id 1 runs from a position before 128 // 8 + 1 to one at or after 256 - 128 // 8 - 1.
All inputs are finite; a program needn't handle non-finite values.
Results may differ from a plain program's by a relative error of at most 0.02.
Values may be sent and summed in bfloat16 or wider, within the bound.
No kernel may reach another device: no remote copies, remote signals or barrier semaphores. Data moves between devices by JAX's collectives and lax.ppermute only.
A program may use at most 192 MiB of HBM per device.

v0:
```python
from functools import partial
import math

import jax
import jax.numpy as jnp
from jax import lax
from jax.sharding import PartitionSpec as P

D = 768
HEADS = 12
HEAD = 64
FF = 3072
ROT = 16
LAYERS = 2


def layer_norm(stream, norm_gain, norm_shift):
    centered = stream - jnp.mean(stream, axis=-1, keepdims=True)
    spread = jnp.mean(centered * centered, axis=-1, keepdims=True)
    return centered * lax.rsqrt(spread + 1e-05) * norm_gain + norm_shift


def both_norms(stream, gain_attn, shift_attn, gain_mlp, shift_mlp):
    return (layer_norm(stream, gain_attn, shift_attn), layer_norm(stream, gain_mlp, shift_mlp))


def angles(positions):
    inverse = 10000.0 ** (-jnp.arange(0, ROT, 2, dtype=jnp.float32) / ROT)
    phases = positions.astype(jnp.float32)[:, None] * inverse[None, :]
    return (jnp.cos(phases)[:, None, :], jnp.sin(phases)[:, None, :])


def rotate(heads_in, cosine_table, sine_table):
    half_rot = cosine_table.shape[-1]
    first_half = heads_in[..., :half_rot]
    second_half = heads_in[..., half_rot : 2 * half_rot]
    untouched = heads_in[..., 2 * half_rot :]
    return jnp.concatenate(
        [
            first_half * cosine_table - second_half * sine_table,
            second_half * cosine_table + first_half * sine_table,
            untouched,
        ],
        axis=-1,
    )


def split_blocks(update, running, key_piece, value_piece, offset):
    piece_rows = key_piece.shape[0]
    block_rows = 512 if piece_rows > 512 and piece_rows % 512 == 0 else piece_rows
    block_count = piece_rows // block_rows
    if block_count == 1:
        return update(running, key_piece, value_piece, offset)

    def advance(state, inputs):
        key_block, value_block, start = inputs
        return (update(state, key_block, value_block, offset + start), None)

    starts = jnp.arange(block_count, dtype=jnp.int32) * block_rows
    state, _ = lax.scan(
        advance,
        running,
        (
            key_piece.reshape(block_count, block_rows, -1),
            value_piece.reshape(block_count, block_rows, -1),
            starts,
        ),
    )
    return state


def stack_layers(per_layer, member):
    return jnp.stack([layer_entry[member] for layer_entry in per_layer])


def flatten_rows(matrix):
    return matrix.reshape(matrix.shape[:-2] + (-1, 128))


def local(
    tokens,
    segment_ids,
    cotangent,
    qkv_weight,
    qkv_bias,
    attn_weight,
    attn_bias,
    up_weight,
    up_bias,
    down_weight,
    down_bias,
    attn_gain,
    attn_shift,
    mlp_gain,
    mlp_shift,
):
    tok_rows = tokens.shape[0]
    group_rows = tok_rows * lax.axis_size("cp")
    score_scale = 1.0 / math.sqrt(HEAD)
    all_segments = lax.all_gather(segment_ids, "cp", axis=0, tiled=True)
    row_index = lax.axis_index("cp") * tok_rows + jnp.arange(tok_rows, dtype=jnp.int32)
    positions = row_index - jnp.sum(
        (all_segments[None, :] < segment_ids[:, None]).astype(jnp.int32), axis=1
    )
    cosine_table, sine_table = angles(positions)

    def visible_mask(offset, block_rows):
        key_index = offset + jnp.arange(block_rows, dtype=jnp.int32)
        key_segment = lax.dynamic_slice_in_dim(all_segments, offset, block_rows)
        return (key_index[None, :] <= row_index[:, None]) & (
            key_segment[None, :] == segment_ids[:, None]
        )

    def online_step(query_heads, running, key_block, value_block, offset):
        row_max, denominator, weighted = running
        block_rows = key_block.shape[0]
        key_heads = key_block.reshape(block_rows, HEADS, HEAD)
        value_heads = value_block.reshape(block_rows, HEADS, HEAD)
        scores = (
            jnp.einsum("qhd,khd->hqk", query_heads, key_heads, preferred_element_type=jnp.float32)
            * score_scale
        )
        visible = visible_mask(offset, block_rows)
        scores = jnp.where(visible[None], scores, -1e30)
        new_max = jnp.maximum(row_max, jnp.max(scores, axis=-1))
        rescale = jnp.exp(row_max - new_max)
        weights = jnp.where(visible[None], jnp.exp(scores - new_max[..., None]), 0.0)
        denominator = denominator * rescale + jnp.sum(weights, axis=-1)
        weighted = weighted * rescale[..., None] + jnp.einsum(
            "hqk,khd->hqd",
            weights.astype(jnp.bfloat16),
            value_heads,
            preferred_element_type=jnp.float32,
        )
        return (new_max, denominator, weighted)

    stream = tokens.astype(jnp.float32)
    stored = []
    for depth in range(LAYERS):
        params = (
            lax.all_gather(qkv_weight[depth], ("dp", "cp"), axis=0, tiled=True),
            lax.all_gather(qkv_bias[depth], ("dp", "cp"), axis=0, tiled=True),
            lax.all_gather(attn_weight[depth], ("dp", "cp"), axis=0, tiled=True),
            lax.all_gather(attn_bias[depth], ("dp", "cp"), axis=0, tiled=True),
            lax.all_gather(up_weight[depth], ("dp", "cp"), axis=0, tiled=True),
            lax.all_gather(up_bias[depth], ("dp", "cp"), axis=0, tiled=True),
            lax.all_gather(down_weight[depth], ("dp", "cp"), axis=0, tiled=True),
            lax.all_gather(down_bias[depth], ("dp", "cp"), axis=0, tiled=True),
            lax.all_gather(attn_gain[depth], ("dp", "cp"), axis=0, tiled=True),
            lax.all_gather(attn_shift[depth], ("dp", "cp"), axis=0, tiled=True),
            lax.all_gather(mlp_gain[depth], ("dp", "cp"), axis=0, tiled=True),
            lax.all_gather(mlp_shift[depth], ("dp", "cp"), axis=0, tiled=True),
        )
        (
            proj_qkv,
            bias_qkv,
            proj_attn,
            bias_attn,
            proj_up,
            bias_up,
            proj_down,
            bias_down,
            gain_attn,
            shift_attn,
            gain_mlp,
            shift_mlp,
        ) = params
        normed_attn, normed_mlp = both_norms(
            stream,
            gain_attn.astype(jnp.float32),
            shift_attn.astype(jnp.float32),
            gain_mlp.astype(jnp.float32),
            shift_mlp.astype(jnp.float32),
        )
        normed_attn = normed_attn.astype(jnp.bfloat16)
        normed_mlp = normed_mlp.astype(jnp.bfloat16)
        projected = jnp.dot(
            normed_attn, proj_qkv, preferred_element_type=jnp.float32
        ) + bias_qkv.astype(jnp.float32)
        queries = rotate(
            projected[:, :D].reshape(tok_rows, HEADS, HEAD), cosine_table, sine_table
        ).astype(jnp.bfloat16)
        key_rows = (
            rotate(projected[:, D : 2 * D].reshape(tok_rows, HEADS, HEAD), cosine_table, sine_table)
            .astype(jnp.bfloat16)
            .reshape(tok_rows, D)
        )
        values = projected[:, 2 * D :].astype(jnp.bfloat16)
        initial = (
            jnp.full((HEADS, tok_rows), -1e30, jnp.float32),
            jnp.zeros((HEADS, tok_rows), jnp.float32),
            jnp.zeros((HEADS, tok_rows, HEAD), jnp.float32),
        )
        row_max, denominator, weighted = split_blocks(
            partial(online_step, queries),
            initial,
            lax.all_gather(key_rows, "cp", axis=0, tiled=True),
            lax.all_gather(values, "cp", axis=0, tiled=True),
            jnp.int32(0),
        )
        attended = jnp.transpose(weighted / denominator[..., None], (1, 0, 2)).reshape(tok_rows, D)
        log_total = row_max + jnp.log(denominator)
        attended_low = attended.astype(jnp.bfloat16)
        attn_branch = jnp.dot(
            attended_low, proj_attn, preferred_element_type=jnp.float32
        ) + bias_attn.astype(jnp.float32)
        hidden_pre = jnp.dot(
            normed_mlp, proj_up, preferred_element_type=jnp.float32
        ) + bias_up.astype(jnp.float32)
        hidden = jax.nn.gelu(hidden_pre, approximate=False).astype(jnp.bfloat16)
        mlp_branch = jnp.dot(
            hidden, proj_down, preferred_element_type=jnp.float32
        ) + bias_down.astype(jnp.float32)
        stored.append(
            (
                stream,
                normed_attn,
                normed_mlp,
                queries,
                key_rows,
                values,
                attended,
                attended_low,
                log_total,
                hidden_pre,
                hidden,
            )
        )
        stream = stream + attn_branch + mlp_branch
    grad_stream = cotangent.astype(jnp.float32)
    per_layer = [None] * LAYERS
    for depth in reversed(range(LAYERS)):
        (
            saved_stream,
            normed_attn,
            normed_mlp,
            queries,
            key_rows,
            values,
            attended,
            attended_low,
            log_total,
            hidden_pre,
            hidden,
        ) = stored[depth]
        params = (
            lax.all_gather(qkv_weight[depth], ("dp", "cp"), axis=0, tiled=True),
            lax.all_gather(qkv_bias[depth], ("dp", "cp"), axis=0, tiled=True),
            lax.all_gather(attn_weight[depth], ("dp", "cp"), axis=0, tiled=True),
            lax.all_gather(attn_bias[depth], ("dp", "cp"), axis=0, tiled=True),
            lax.all_gather(up_weight[depth], ("dp", "cp"), axis=0, tiled=True),
            lax.all_gather(up_bias[depth], ("dp", "cp"), axis=0, tiled=True),
            lax.all_gather(down_weight[depth], ("dp", "cp"), axis=0, tiled=True),
            lax.all_gather(down_bias[depth], ("dp", "cp"), axis=0, tiled=True),
            lax.all_gather(attn_gain[depth], ("dp", "cp"), axis=0, tiled=True),
            lax.all_gather(attn_shift[depth], ("dp", "cp"), axis=0, tiled=True),
            lax.all_gather(mlp_gain[depth], ("dp", "cp"), axis=0, tiled=True),
            lax.all_gather(mlp_shift[depth], ("dp", "cp"), axis=0, tiled=True),
        )
        (
            proj_qkv,
            bias_qkv,
            proj_attn,
            bias_attn,
            proj_up,
            bias_up,
            proj_down,
            bias_down,
            gain_attn,
            shift_attn,
            gain_mlp,
            shift_mlp,
        ) = params
        grad_low = grad_stream.astype(jnp.bfloat16)
        bias_grad = jnp.sum(grad_low.astype(jnp.float32), axis=0)
        attn_weight_grad = jnp.einsum(
            "td,te->de", attended_low, grad_low, preferred_element_type=jnp.float32
        )
        down_weight_grad = jnp.einsum(
            "tf,te->fe", hidden, grad_low, preferred_element_type=jnp.float32
        )
        grad_attended = jnp.einsum(
            "te,de->td", grad_low, proj_attn, preferred_element_type=jnp.float32
        ).astype(jnp.bfloat16)
        grad_hidden = jnp.einsum(
            "te,fe->tf", grad_low, proj_down, preferred_element_type=jnp.float32
        )
        _, gelu_pull = jax.vjp(partial(jax.nn.gelu, approximate=False), hidden_pre)
        grad_pre = gelu_pull(grad_hidden)[0].astype(jnp.bfloat16)
        up_weight_grad = jnp.einsum(
            "td,tf->df", normed_mlp, grad_pre, preferred_element_type=jnp.float32
        )
        up_bias_grad = jnp.sum(grad_pre.astype(jnp.float32), axis=0)
        grad_normed_mlp = jnp.einsum(
            "tf,df->td", grad_pre, proj_up, preferred_element_type=jnp.float32
        )
        all_keys, all_values = (
            lax.all_gather(key_rows, "cp", axis=0, tiled=True),
            lax.all_gather(values, "cp", axis=0, tiled=True),
        )
        grad_heads = grad_attended.reshape(tok_rows, HEADS, HEAD)
        row_dot = jnp.transpose(
            jnp.sum(
                grad_heads.astype(jnp.float32) * attended.reshape(tok_rows, HEADS, HEAD), axis=-1
            )
        )
        block_rows = 512 if group_rows > 512 and group_rows % 512 == 0 else group_rows
        block_count = group_rows // block_rows
        starts = jnp.arange(block_count, dtype=jnp.int32) * block_rows

        def back_step(grad_query, inputs):
            key_block, value_block, offset = inputs
            key_heads = key_block.reshape(block_rows, HEADS, HEAD)
            value_heads = value_block.reshape(block_rows, HEADS, HEAD)
            scores = (
                jnp.einsum("qhd,khd->hqk", queries, key_heads, preferred_element_type=jnp.float32)
                * score_scale
            )
            visible = visible_mask(offset, block_rows)
            weights = jnp.where(visible[None], jnp.exp(scores - log_total[..., None]), 0.0)
            grad_weights = jnp.einsum(
                "qhd,khd->hqk", grad_heads, value_heads, preferred_element_type=jnp.float32
            )
            grad_scores = (weights * (grad_weights - row_dot[..., None])).astype(jnp.bfloat16)
            grad_query = grad_query + jnp.einsum(
                "hqk,khd->hqd", grad_scores, key_heads, preferred_element_type=jnp.float32
            )
            key_grad = (
                jnp.einsum("hqk,qhd->khd", grad_scores, queries, preferred_element_type=jnp.float32)
                * score_scale
            )
            value_grad = jnp.einsum(
                "hqk,qhd->khd",
                weights.astype(jnp.bfloat16),
                grad_heads,
                preferred_element_type=jnp.float32,
            )
            return (
                grad_query,
                (key_grad.reshape(block_rows, D), value_grad.reshape(block_rows, D)),
            )

        grad_query, (key_grads, value_grads) = lax.scan(
            back_step,
            jnp.zeros((HEADS, tok_rows, HEAD), jnp.float32),
            (
                all_keys.reshape(block_count, block_rows, D),
                all_values.reshape(block_count, block_rows, D),
                starts,
            ),
        )
        local_key_grad, local_value_grad = (
            lax.psum_scatter(
                key_grads.reshape(group_rows, D).astype(jnp.bfloat16),
                "cp",
                scatter_dimension=0,
                tiled=True,
            ).astype(jnp.float32),
            lax.psum_scatter(
                value_grads.reshape(group_rows, D).astype(jnp.bfloat16),
                "cp",
                scatter_dimension=0,
                tiled=True,
            ).astype(jnp.float32),
        )
        query_raw = rotate(
            jnp.transpose(grad_query * score_scale, (1, 0, 2)), cosine_table, -sine_table
        )
        key_raw = rotate(local_key_grad.reshape(tok_rows, HEADS, HEAD), cosine_table, -sine_table)
        grad_projected = jnp.concatenate(
            [query_raw.reshape(tok_rows, D), key_raw.reshape(tok_rows, D), local_value_grad], axis=1
        ).astype(jnp.bfloat16)
        qkv_weight_grad = jnp.einsum(
            "td,te->de", normed_attn, grad_projected, preferred_element_type=jnp.float32
        )
        qkv_bias_grad = jnp.sum(grad_projected.astype(jnp.float32), axis=0)
        grad_normed_attn = jnp.einsum(
            "te,de->td", grad_projected, proj_qkv, preferred_element_type=jnp.float32
        )
        _, norm_pull = jax.vjp(
            both_norms,
            saved_stream,
            gain_attn.astype(jnp.float32),
            shift_attn.astype(jnp.float32),
            gain_mlp.astype(jnp.float32),
            shift_mlp.astype(jnp.float32),
        )
        grad_input, attn_gain_grad, attn_shift_grad, mlp_gain_grad, mlp_shift_grad = norm_pull(
            (grad_normed_attn, grad_normed_mlp)
        )
        grad_stream = grad_stream + grad_input
        summed = (
            lax.psum_scatter(
                flatten_rows(qkv_weight_grad), ("dp", "cp"), scatter_dimension=0, tiled=True
            ),
            lax.psum_scatter(qkv_bias_grad, ("dp", "cp"), scatter_dimension=0, tiled=True),
            lax.psum_scatter(
                flatten_rows(attn_weight_grad), ("dp", "cp"), scatter_dimension=0, tiled=True
            ),
            lax.psum_scatter(bias_grad, ("dp", "cp"), scatter_dimension=0, tiled=True),
            lax.psum_scatter(
                flatten_rows(up_weight_grad), ("dp", "cp"), scatter_dimension=0, tiled=True
            ),
            lax.psum_scatter(up_bias_grad, ("dp", "cp"), scatter_dimension=0, tiled=True),
            lax.psum_scatter(
                flatten_rows(down_weight_grad), ("dp", "cp"), scatter_dimension=0, tiled=True
            ),
            lax.psum_scatter(bias_grad, ("dp", "cp"), scatter_dimension=0, tiled=True),
            lax.psum_scatter(attn_gain_grad, ("dp", "cp"), scatter_dimension=0, tiled=True),
            lax.psum_scatter(attn_shift_grad, ("dp", "cp"), scatter_dimension=0, tiled=True),
            lax.psum_scatter(mlp_gain_grad, ("dp", "cp"), scatter_dimension=0, tiled=True),
            lax.psum_scatter(mlp_shift_grad, ("dp", "cp"), scatter_dimension=0, tiled=True),
        )
        per_layer[depth] = (
            summed[0].reshape(-1, 3 * D),
            summed[1],
            summed[2].reshape(-1, D),
            summed[3],
            summed[4].reshape(-1, FF),
            summed[5],
            summed[6].reshape(-1, D),
            summed[7],
            summed[8],
            summed[9],
            summed[10],
            summed[11],
        )
    stacked = [stack_layers(per_layer, member) for member in range(12)]
    return (
        stream.astype(jnp.bfloat16),
        grad_stream,
        stacked[0],
        stacked[1],
        stacked[2],
        stacked[3],
        stacked[4],
        stacked[5],
        stacked[6],
        stacked[7],
        stacked[8],
        stacked[9],
        stacked[10],
        stacked[11],
    )


def solution(mesh):
    in_specs = (
        P(("dp", "cp"), None),
        P(("dp", "cp")),
        P(("dp", "cp"), None),
        P(None, ("dp", "cp"), None),
        P(None, ("dp", "cp")),
        P(None, ("dp", "cp"), None),
        P(None, ("dp", "cp")),
        P(None, ("dp", "cp"), None),
        P(None, ("dp", "cp")),
        P(None, ("dp", "cp"), None),
        P(None, ("dp", "cp")),
        P(None, ("dp", "cp")),
        P(None, ("dp", "cp")),
        P(None, ("dp", "cp")),
        P(None, ("dp", "cp")),
    )
    out_specs = (
        P(("dp", "cp"), None),
        P(("dp", "cp"), None),
        P(None, ("dp", "cp"), None),
        P(None, ("dp", "cp")),
        P(None, ("dp", "cp"), None),
        P(None, ("dp", "cp")),
        P(None, ("dp", "cp"), None),
        P(None, ("dp", "cp")),
        P(None, ("dp", "cp"), None),
        P(None, ("dp", "cp")),
        P(None, ("dp", "cp")),
        P(None, ("dp", "cp")),
        P(None, ("dp", "cp")),
        P(None, ("dp", "cp")),
    )
    return jax.shard_map(local, mesh=mesh, in_specs=in_specs, out_specs=out_specs, check_vma=False)
```

profile of v0, /device:TPU:5, one launch (start us, length us, event | category | flops | bytes accessed | tf_op | source)
XLA Modules:
  0.0 1756.4 jit_solution(7130277607074099972)
XLA Ops:
  23.3 42.1 %all-reduce.31 = (bf16[3072]{0:T(1024)(128)(2,1)}, bf16[3072]{0:T(1024)(128)(2,1)S(1)}, bf16[768]{0:T(1024)(128)(2,1)S(1)}, bf16[768]{0:T(1024)(128)(2,1)S(1)}, ...) all-reduce(bf16[3072]{0:T(1024)(128)(2,1)S(1)} %dynamic-update-slic, ...), channel_id=23, replica_groups=mesh['dp'=16,'cp'=2] {'dp','cp'}, use_global_device_ids=true, to_apply=%add.14 | all-reduce | flops 19968 | bytes 79872
  70.7 59.4 %all-gather.34.cloned.1.call-done = bf16[1,768,2304]{2,1,0:T(8,128)(2,1)} async-done(((bf16[1,24,2304]{2,1,0:T(8,128)(2,1)}), bf16[1,768,2304]{2,1,0:T(8,128)(2,1)}) %all-gather.34.cloned.1.call-update) | async-done | bytes 3538960 | tf_op jit(solution)/shard_map/all_gather | solution.py:141
  133.2 6.9 all_gather.109
  140.6 7.4 all_gather.108
  151.9 44.2 %all-gather.38.cloned.1.call-done = bf16[1,768,3072]{2,1,0:T(8,128)(2,1)} async-done(((bf16[1,24,3072]{2,1,0:T(8,128)(2,1)}), bf16[1,768,3072]{2,1,0:T(8,128)(2,1)}) %all-gather.38.cloned.1.call-update) | async-done | bytes 4718608 | tf_op jit(solution)/shard_map/all_gather | solution.py:145
  196.1 8.4 multiply_convert_fusion.3
  204.5 57.4 %all-gather.40.cloned.1.call-done = bf16[1,3072,768]{2,1,0:T(8,128)(2,1)} async-done(((bf16[1,96,768]{2,1,0:T(8,128)(2,1)}), bf16[1,3072,768]{2,1,0:T(8,128)(2,1)}) %all-gather.40.cloned.1.call-update) | async-done | bytes 4718608 | tf_op jit(solution)/shard_map/all_gather | solution.py:147
  265.0 53.2 %all-gather.36.cloned.1.call-done = bf16[1,768,768]{2,1,0:T(8,128)(2,1)} async-done(((bf16[1,24,768]{2,1,0:T(8,128)(2,1)}), bf16[1,768,768]{2,1,0:T(8,128)(2,1)}) %all-gather.36.cloned.1.call-update) | async-done | bytes 1179664 | tf_op jit(solution)/shard_map/all_gather | solution.py:143
  320.2 60.5 %all-gather.42.cloned.1.call-done = bf16[1,768,2304]{2,1,0:T(8,128)(2,1)} async-done(((bf16[1,24,2304]{2,1,0:T(8,128)(2,1)}), bf16[1,768,2304]{2,1,0:T(8,128)(2,1)}) %all-gather.42.cloned.1.call-update) | async-done | bytes 3538960 | tf_op jit(solution)/shard_map/all_gather | solution.py:141
  384.4 6.9 all_gather.123
  392.5 6.3 all_gather.122
  418.0 28.1 %all-gather.46.cloned.1.call-done = bf16[1,768,3072]{2,1,0:T(8,128)(2,1)} async-done(((bf16[1,24,3072]{2,1,0:T(8,128)(2,1)}), bf16[1,768,3072]{2,1,0:T(8,128)(2,1)}) %all-gather.46.cloned.1.call-update) | async-done | bytes 4718608 | tf_op jit(solution)/shard_map/all_gather | solution.py:145
  446.1 8.5 multiply_convert_fusion.2
  454.7 56.8 %all-gather.48.cloned.1.call-done = bf16[1,3072,768]{2,1,0:T(8,128)(2,1)} async-done(((bf16[1,96,768]{2,1,0:T(8,128)(2,1)}), bf16[1,3072,768]{2,1,0:T(8,128)(2,1)}) %all-gather.48.cloned.1.call-update) | async-done | bytes 4718608 | tf_op jit(solution)/shard_map/all_gather | solution.py:147
  517.1 8.2 reduce-scatter.37.cloned.1.call-done
  528.1 13.1 reduce-scatter.39.cloned.1.call-done
  574.8 10.4 reduce-scatter.43.cloned.1.call-done
  605.1 7.9 reshape.517
  618.2 7.9 reshape.516
  632.4 10.9 reshape.521
  649.5 10.8 reshape.523
  666.5 10.9 reshape.520
  683.7 10.7 reshape.522
  699.4 26.5 %all-reduce.34.cloned.1.call-done = (f32[2304]{0:T(1024)}, f32[2304]{0:T(1024)}, f32[768]{0:T(1024)}, f32[768]{0:T(1024)}, f32[3072]{0:T(1024)}, /*index=5*/f32[...) async-done(((f32[2304]{0:T(1024)}, f32[2304]{0:T(1024)}, ...) | async-done | bytes 73744
  739.9 90.7 %reduce-scatter.27.cloned.1.call-done = f32[144,128]{1,0:T(8,128)} async-done(((f32[4608,128]{1,0:T(8,128)}), f32[144,128]{1,0:T(8,128)}) %reduce-scatter.27.cloned.1.call-update) | async-done | bytes 73744 | tf_op jit(solution)/shard_map/reduce_scatter | solution.py:397
  831.5 103.1 %reduce-scatter.25.cloned.1.call-done = f32[144,128]{1,0:T(8,128)} async-done(((f32[4608,128]{1,0:T(8,128)}), f32[144,128]{1,0:T(8,128)}) %reduce-scatter.25.cloned.1.call-update) | async-done | bytes 73744 | tf_op jit(solution)/shard_map/reduce_scatter | solution.py:397
  936.1 122.1 %reduce-scatter.23.cloned.1.call-done = f32[432,128]{1,0:T(8,128)} async-done(((f32[13824,128]{1,0:T(8,128)}), f32[432,128]{1,0:T(8,128)}) %reduce-scatter.23.cloned.1.call-update) | async-done | bytes 221200 | tf_op jit(solution)/shard_map/reduce_scatter | solution.py:393
  1059.2 124.0 %reduce-scatter.21.cloned.1.call-done = f32[432,128]{1,0:T(8,128)} async-done(((f32[13824,128]{1,0:T(8,128)}), f32[432,128]{1,0:T(8,128)}) %reduce-scatter.21.cloned.1.call-update) | async-done | bytes 221200 | tf_op jit(solution)/shard_map/reduce_scatter | solution.py:393
  1185.0 138.5 %reduce-scatter.31.cloned.1.call-done = f32[576,128]{1,0:T(8,128)} async-done(((f32[18432,128]{1,0:T(8,128)}), f32[576,128]{1,0:T(8,128)}) %reduce-scatter.31.cloned.1.call-update) | async-done | bytes 294928 | tf_op jit(solution)/shard_map/reduce_scatter | solution.py:401
  1324.5 140.5 %reduce-scatter.35.cloned.1.call-done = f32[576,128]{1,0:T(8,128)} async-done(((f32[18432,128]{1,0:T(8,128)}), f32[576,128]{1,0:T(8,128)}) %reduce-scatter.35.cloned.1.call-update) | async-done | bytes 294928 | tf_op jit(solution)/shard_map/reduce_scatter | solution.py:405
  1466.0 139.3 %reduce-scatter.29.cloned.1.call-done = f32[576,128]{1,0:T(8,128)} async-done(((f32[18432,128]{1,0:T(8,128)}), f32[576,128]{1,0:T(8,128)}) %reduce-scatter.29.cloned.1.call-update) | async-done | bytes 294928 | tf_op jit(solution)/shard_map/reduce_scatter | solution.py:401
  1607.2 139.6 %reduce-scatter.33.cloned.1.call-done = f32[576,128]{1,0:T(8,128)} async-done(((f32[18432,128]{1,0:T(8,128)}), f32[576,128]{1,0:T(8,128)}) %reduce-scatter.33.cloned.1.call-update) | async-done | bytes 294928 | tf_op jit(solution)/shard_map/reduce_scatter | solution.py:405
  (462 shorter events, 178.8 us)
Async XLA Ops:
  7.3 60.8 %all-gather.44.cloned.1.call-start = ((), (), s32[]{:S(2)}) async-start(), calls=%async_computation.25 | async-start | bytes 1216512 | tf_op jit(solution)/shard_map/all_gather | solution.py:143
  8.9 121.2 %all-gather.34.cloned.1.call-start = ((), (), s32[]{:S(2)}) async-start(), calls=%async_computation.20 | async-start | bytes 3649536 | tf_op jit(solution)/shard_map/all_gather | solution.py:141
  10.7 185.4 %all-gather.38.cloned.1.call-start = ((), (), s32[]{:S(2)}) async-start(), calls=%async_computation.22 | async-start | bytes 4866048 | tf_op jit(solution)/shard_map/all_gather | solution.py:145
  12.5 249.4 %all-gather.40.cloned.1.call-start = ((), (), s32[]{:S(2)}) async-start(), calls=%async_computation.23 | async-start | bytes 4866048 | tf_op jit(solution)/shard_map/all_gather | solution.py:147
  13.3 304.9 %all-gather.36.cloned.1.call-start = ((), (), s32[]{:S(2)}) async-start(), calls=%async_computation.21 | async-start | bytes 1216512 | tf_op jit(solution)/shard_map/all_gather | solution.py:143
  13.9 366.8 %all-gather.42.cloned.1.call-start = ((), (), s32[]{:S(2)}) async-start(), calls=%async_computation.24 | async-start | bytes 3649536 | tf_op jit(solution)/shard_map/all_gather | solution.py:141
  14.4 431.7 %all-gather.46.cloned.1.call-start = ((), (), s32[]{:S(2)}) async-start(), calls=%async_computation.26 | async-start | bytes 4866048 | tf_op jit(solution)/shard_map/all_gather | solution.py:145
  15.2 496.3 %all-gather.48.cloned.1.call-start = ((), (), s32[]{:S(2)}) async-start(), calls=%async_computation.27 | async-start | bytes 4866048 | tf_op jit(solution)/shard_map/all_gather | solution.py:147
  15.9 509.3 %reduce-scatter.37.cloned.1.call-start = ((), (), s32[]{:S(2)}) async-start(), calls=%async_computation.28 | async-start | bytes 589824
  16.1 179.9 %copy-start.70 = (f32[128]{0:T(128)}, f32[128]{0:T(128)S(1)}, u32[]{:S(2)}) copy-start(f32[128]{0:T(128)S(1)} %broadcast_multiply_fusion.1) | copy-start | bytes 1540
  16.3 116.5 %copy-start.92 = (f32[128]{0:T(128)}, f32[128]{0:T(128)S(1)}, u32[]{:S(2)}) copy-start(f32[128]{0:T(128)S(1)} %fusion.117) | copy-start | bytes 1540
  16.4 179.7 %copy-start.77 = (f32[128]{0:T(128)}, f32[128]{0:T(128)S(1)}, u32[]{:S(2)}) copy-start(f32[128]{0:T(128)S(1)} %fusion.124) | copy-start | bytes 1540
  65.4 130.7 %copy-start.54 = (f32[768]{0:T(1024)}, f32[768]{0:T(1024)S(1)}, u32[]{:S(2)}) copy-start(f32[768]{0:T(1024)S(1)} %convert_element_type.301) | copy-start | bytes 9220
  65.4 315.3 %copy-start.52 = (f32[768]{0:T(1024)}, f32[768]{0:T(1024)S(1)}, u32[]{:S(2)}) copy-start(f32[768]{0:T(1024)S(1)} %convert_element_type.305) | copy-start | bytes 9220
  67.9 72.6 %copy-start.68 = (f32[128,8]{0,1:T(8,128)}, f32[128,8]{0,1:T(8,128)S(1)}, u32[]{:S(2)}) copy-start(f32[128,8]{0,1:T(8,128)S(1)} %get-tuple-element.203) | copy-start | bytes 12292
  68.0 82.6 %copy-start.36 = (pred[128,256]{1,0:T(8,128)(4,1)}, pred[128,256]{1,0:T(8,128)(4,1)S(1)}, u32[]{:S(2)}) copy-start(pred[128,256]{1,0:T(8,128)(4,1)S(1)} %fusion.120) | copy-start | bytes 98308
  151.9 166.3 %copy-start.44 = (bf16[128,12,64]{0,2,1:T(8,128)(2,1)}, bf16[128,12,64]{0,2,1:T(8,128)(2,1)S(1)}, u32[]{:S(2)}) copy-start(bf16[128,12,64]{0,2,1:T(8,128)(2,1)S(1)} %get-tuple-element.224) | copy-start | bytes 589828
  151.9 110.0 %copy-start.84 = (f32[768]{0:T(1024)S(1)}, f32[768]{0:T(1024)}, u32[]{:S(2)}) copy-start(f32[768]{0:T(1024)} %convert_element_type.303) | copy-start | bytes 9220
  407.7 133.5 %reduce-scatter.39.cloned.1.call-start = ((), (), s32[]{:S(2)}) async-start(), calls=%async_computation.29 | async-start | bytes 589824
  417.5 94.0 %copy-start.4 = (bf16[128,768]{1,0:T(8,128)(2,1)S(1)}, bf16[128,768]{1,0:T(8,128)(2,1)}, u32[]{:S(2)}) copy-start(bf16[128,768]{1,0:T(8,128)(2,1)} %param.17) | copy-start | bytes 589828
  417.5 155.2 %reduce-scatter.41.cloned.1.call-start = ((), (), s32[]{:S(2)}) async-start(), calls=%async_computation.30 | async-start | bytes 589824
  556.0 29.2 %reduce-scatter.43.cloned.1.call-start = ((), (), s32[]{:S(2)}) async-start(), calls=%async_computation.31 | async-start | bytes 589824
  562.4 163.4 %all-reduce.34.cloned.1.call-start = ((), (), s32[]{:S(2)}) async-start(), calls=%async_computation.32 | async-start | bytes 180224
  594.0 236.6 %reduce-scatter.27.cloned.1.call-start = ((), (), s32[]{:S(2)}) async-start(), calls=%async_computation.15 | async-start | bytes 2433024 | tf_op jit(solution)/shard_map/reduce_scatter | solution.py:397
  597.0 337.6 %reduce-scatter.25.cloned.1.call-start = ((), (), s32[]{:S(2)}) async-start(), calls=%async_computation.14 | async-start | bytes 2433024 | tf_op jit(solution)/shard_map/reduce_scatter | solution.py:397
  600.0 458.2 %reduce-scatter.23.cloned.1.call-start = ((), (), s32[]{:S(2)}) async-start(), calls=%async_computation.13 | async-start | bytes 7299072 | tf_op jit(solution)/shard_map/reduce_scatter | solution.py:393
  613.1 570.0 %reduce-scatter.21.cloned.1.call-start = ((), (), s32[]{:S(2)}) async-start(), calls=%async_computation.12 | async-start | bytes 7299072 | tf_op jit(solution)/shard_map/reduce_scatter | solution.py:393
  626.2 697.3 %reduce-scatter.31.cloned.1.call-start = ((), (), s32[]{:S(2)}) async-start(), calls=%async_computation.17 | async-start | bytes 9732096 | tf_op jit(solution)/shard_map/reduce_scatter | solution.py:401
  643.4 821.6 %reduce-scatter.35.cloned.1.call-start = ((), (), s32[]{:S(2)}) async-start(), calls=%async_computation.19 | async-start | bytes 9732096 | tf_op jit(solution)/shard_map/reduce_scatter | solution.py:405
  660.2 945.1 %reduce-scatter.29.cloned.1.call-start = ((), (), s32[]{:S(2)}) async-start(), calls=%async_computation.16 | async-start | bytes 9732096 | tf_op jit(solution)/shard_map/reduce_scatter | solution.py:401
  677.5 1069.4 %reduce-scatter.33.cloned.1.call-start = ((), (), s32[]{:S(2)}) async-start(), calls=%async_computation.18 | async-start | bytes 9732096 | tf_op jit(solution)/shard_map/reduce_scatter | solution.py:405
  727.4 1021.4 %copy-start.86 = (f32[2,24]{1,0:T(2,128)}, f32[2,24]{1,0:T(2,128)S(1)}, u32[]{:S(2)}) copy-start(f32[2,24]{1,0:T(2,128)S(1)} %pad_maximum_fusion.19) | copy-start | bytes 580
  (95 other events, 1085.0 us)
Sparse Core Ops, SparseCore 0:
  11.6 55.9 all-gather.43
  71.1 59.0 all-gather.33
  133.7 62.3 all-gather.37
  199.4 62.4 all-gather.39
  265.2 52.9 all-gather.35
  321.6 59.0 all-gather.41
  383.6 62.4 all-gather.45
  449.0 62.4 all-gather.47
  513.7 11.4 reduce-scatter.36
  528.0 13.1 reduce-scatter.38
  556.2 13.1 reduce-scatter.40
  572.1 13.1 reduce-scatter.42
  594.1 131.6 all-reduce.33
  731.0 99.5 reduce-scatter.26
  836.6 97.9 reduce-scatter.24
  940.1 118.0 reduce-scatter.22
  1064.7 118.4 reduce-scatter.20
  1188.9 134.4 reduce-scatter.30
  1330.4 134.5 reduce-scatter.34
  1470.7 134.5 reduce-scatter.28
  1612.3 134.5 reduce-scatter.32
where the time goes:
time: 1770 us; the launch traced here: 1760 us
  waiting for transfers between devices  1420 us (80%)
  local copies, waits for them, and re-layouts  117 us (7%)
  matrix products  106 us (6%)
  blocking collectives  72.8 us (4%)
  other arithmetic  24.4 us (1%)
    reduce_scatter x2, waiting for transfers between devices, local(): lax.psum_scatter(flatten_rows(down_weight_grad), ('dp', 'cp'), scatter_di...  280 us
    reduce_scatter x2, waiting for transfers between devices, local(): lax.psum_scatter(flatten_rows(up_weight_grad), ('dp', 'cp'), scatter_dime...  278 us
    reduce_scatter x2, waiting for transfers between devices, local(): lax.psum_scatter(flatten_rows(qkv_weight_grad), ('dp', 'cp'), scatter_dim...  246 us
    reduce_scatter x2, waiting for transfers between devices, local(): lax.psum_scatter(flatten_rows(attn_weight_grad), ('dp', 'cp'), scatter_di...  194 us
    all_gather x2, waiting for transfers between devices, local(): lax.all_gather(qkv_weight[depth], ('dp', 'cp'), axis=0, tiled=True)  120 us
    all_gather x2, waiting for transfers between devices, local(): lax.all_gather(down_weight[depth], ('dp', 'cp'), axis=0, tiled=True)  114 us
    all_gather x2, waiting for transfers between devices, local(): lax.all_gather(up_weight[depth], ('dp', 'cp'), axis=0, tiled=True)  72.2 us
    reshape x8, local copies, waits for them, and re-layouts, flatten_rows(): return matrix.reshape(matrix.shape[:-2] + (-1, 128))  62.2 us
  transfers between devices with their start and end apart: 21, of which 19 were waited for; matrix products, arithmetic and copies ran while one was open for 12% of the time, Pallas kernels for 0%

commit v1 on v0

--- a/solution.py
+++ b/solution.py
@@ -4,7 +4,9 @@
 import jax
 import jax.numpy as jnp
 from jax import lax
-from jax.sharding import PartitionSpec as P
+from jax.experimental import pallas as pl
+from jax.experimental.pallas import tpu as pltpu
+from jax.sharding import Mesh, PartitionSpec as P
 
 D = 768
 HEADS = 12
@@ -444,7 +446,530 @@
     )
 
 
-def solution(mesh):
+TEAM = 4
+TEAM_AXES = ("core", "x")
+LINE_AXES = ("z", "y")
+MINE = (3 * D) // TEAM
+HCOLS = D // TEAM
+UCOLS = FF // TEAM
+VMEM_BYTES = 56 * 1024 * 1024
+BF = jnp.bfloat16
+F32 = jnp.float32
+
+
+def call(body, out_shape, name, operands, scratch=()):
+    return pl.pallas_call(
+        body,
+        out_shape=out_shape,
+        scratch_shapes=list(scratch),
+        compiler_params=pltpu.CompilerParams(vmem_limit_bytes=VMEM_BYTES),
+        name=name,
+    )(*operands)
+
+
+def shape(dims, kind):
+    return jax.ShapeDtypeStruct(dims, kind)
+
+
+def mm(left, right):
+    return jnp.dot(left, right, preferred_element_type=F32)
+
+
+def mm_t(left, right):
+    return lax.dot_general(left, right, (((1,), (1,)), ((), ())), preferred_element_type=F32)
+
+
+def t_mm(left, right):
+    return lax.dot_general(left, right, (((0,), (0,)), ((), ())), preferred_element_type=F32)
+
+
+def pick(member, slot, pieces, wanted):
+    chosen = pieces[0]
+    for s in range(1, TEAM):
+        chosen = jnp.where((member ^ s) == wanted, pieces[s], chosen)
+    return chosen
+
+
+def pack_body(me_ref, qkv_ref, up_ref, small_ref, *outs):
+    me = me_ref[0]
+    for depth in range(LAYERS):
+        rows = qkv_ref.shape[1]
+        qkv = qkv_ref[depth].astype(F32)
+        up = up_ref[depth].astype(F32)
+        blocks = up.shape[1] // (TEAM * 96)
+        parts = []
+        for p in range(TEAM):
+            up_p = jnp.concatenate(
+                [up[:, 96 * (TEAM * b + p) : 96 * (TEAM * b + p + 1)] for b in range(blocks)], axis=1
+            )
+            qkv_p = jnp.concatenate(
+                [qkv[:, D * t + HCOLS * p : D * t + HCOLS * (p + 1)] for t in range(3)]
+                + [jnp.zeros((rows, UCOLS - MINE), F32)],
+                axis=1,
+            )
+            parts.append(jnp.concatenate([up_p, qkv_p], axis=0))
+        small = small_ref[depth].astype(F32)
+        for s in range(TEAM):
+            dest = me ^ s
+            chosen = parts[0]
+            for p in range(1, TEAM):
+                chosen = jnp.where(dest == p, parts[p], chosen)
+            outs[depth * TEAM + s][...] = jnp.concatenate([chosen, small], axis=0).astype(BF)
+
+
+def assemble_body(me_ref, p0, p1, p2, p3, attn_ref, down_ref, q_ref, m_ref):
+    me = me_ref[0]
+    slots = [r[...].astype(F32) for r in (p0, p1, p2, p3)]
+    ordered = [pick(me, None, slots, p) for p in range(TEAM)]
+    up = jnp.concatenate([piece[0:24] for piece in ordered], axis=0)
+    qkv = jnp.concatenate([piece[24:48] for piece in ordered], axis=0)
+    small = jnp.concatenate([piece[48:56] for piece in ordered], axis=0)
+    q_ref[0:96] = qkv[:, :MINE].astype(BF)
+    q_ref[96:128] = small[:, :MINE].astype(BF)
+    m_ref[0:96] = up.astype(BF)
+    m_ref[96:192] = down_ref[...]
+    m_ref[192:224] = jnp.concatenate(
+        [attn_ref[...].astype(F32), jnp.zeros((8, D), F32)], axis=0
+    ).astype(BF)
+
+
+def norm_parts(stream):
+    centered = stream - jnp.mean(stream, axis=-1, keepdims=True)
+    spread = jnp.mean(centered * centered, axis=-1, keepdims=True)
+    inverse = lax.rsqrt(spread + 1e-05)
+    return centered * inverse, inverse
+
+
+def two_slots(first, second):
+    return jnp.concatenate([first[0:TOK].astype(F32), second[0:TOK].astype(F32)], axis=0)
+
+
+TOK = 128
+PAIR = 2 * TOK
+
+
+def turn(block, cosine, sine):
+    lane = lax.broadcasted_iota(jnp.int32, (block.shape[0], 128), 1) % HEAD
+    tiles = []
+    for t in range(block.shape[1] // 128):
+        tile = block[:, 128 * t : 128 * (t + 1)]
+        swapped = jnp.where(
+            lane < ROT // 2, pltpu.roll(tile, 128 - ROT // 2, 1), pltpu.roll(tile, ROT // 2, 1)
+        )
+        tiles.append(tile * cosine + swapped * sine)
+    return jnp.concatenate(tiles, axis=1)
+
+
+def head_mask(rows, head):
+    lane = lax.broadcasted_iota(jnp.int32, (rows, HCOLS), 1)
+    return (lane >= head * HEAD) & (lane < (head + 1) * HEAD)
+
+
+def attend_body(
+    x0, x1, x2, x3, w_ref, b_ref, vec_ref, cos_ref, sin_ref, mask_ref,
+    a_ref, q_ref, k_ref, v_ref, o_ref,
+):
+    weight = w_ref[:, 0:96, :].reshape(D, MINE)
+    for g, (first, second) in enumerate(((x0, x1), (x2, x3))):
+        rows = pl.ds(PAIR * g, PAIR)
+        scaled, _ = norm_parts(two_slots(first[0:TOK], second[0:TOK]))
+        normed = (scaled * vec_ref[2:3] + vec_ref[3:4]).astype(BF)
+        a_ref[rows, :] = normed
+        projected = mm(normed, weight) + b_ref[...]
+        turned = turn(projected[:, : 2 * HCOLS], cos_ref[rows, :], sin_ref[rows, :])
+        queries = (turned[:, :HCOLS].astype(BF) * 0.125).astype(BF)
+        keys = turned[:, HCOLS:].astype(BF)
+        values = projected[:, 2 * HCOLS :].astype(BF)
+        q_ref[rows, :] = queries
+        k_ref[rows, :] = keys
+        v_ref[rows, :] = values
+        total = jnp.zeros((PAIR, HCOLS), F32)
+        for head in range(HEADS // TEAM):
+            owned = head_mask(PAIR, head)
+            scores = mm_t(jnp.where(owned, queries, jnp.zeros_like(queries)), keys) + mask_ref[g]
+            weights = jnp.exp(scores - jnp.max(scores, axis=-1, keepdims=True))
+            below = jnp.sum(weights, axis=-1, keepdims=True)
+            total = total + jnp.where(owned, mm(weights.astype(BF), values) / below, 0.0)
+        o_ref[rows, :] = total.astype(BF)
+
+
+def attn_rows(w_ref):
+    return w_ref[:, 192:224, :].astype(F32)[:, :24].reshape(HCOLS, D).astype(BF)
+
+
+def gelu_parts(u):
+    cdf = 0.5 * (1.0 + lax.erf(u * (1.0 / math.sqrt(2.0))))
+    density = jnp.exp(-0.5 * u * u) * (1.0 / math.sqrt(2.0 * math.pi))
+    return u * cdf, cdf + u * density
+
+
+def mlp_body(x0, x1, x2, x3, w_ref, b_ref, vec_ref, o_ref, c_ref, u_ref, y0, y1, y2, y3):
+    up = w_ref[:, 0:96, :].reshape(D, UCOLS)
+    down = w_ref[:, 96:192, :].reshape(UCOLS, D)
+    attn = attn_rows(w_ref)
+    for g, (first, second, y_first, y_second) in enumerate(((x0, x1, y0, y1), (x2, x3, y2, y3))):
+        rows = pl.ds(PAIR * g, PAIR)
+        scaled, _ = norm_parts(two_slots(first[0:TOK], second[0:TOK]))
+        normed = (scaled * vec_ref[4:5] + vec_ref[5:6]).astype(BF)
+        c_ref[rows, :] = normed
+        before = mm(normed, up) + b_ref[...]
+        u_ref[rows, :] = before
+        hidden = (before * (0.5 * (1.0 + lax.erf(before * (1.0 / math.sqrt(2.0)))))).astype(BF)
+        result = mm(hidden, down) + mm(o_ref[rows, :], attn)
+        y_first[...] = result[0:TOK].astype(y_first.dtype)
+        y_second[...] = result[TOK:].astype(y_second.dtype)
+
+
+def mlp_back_body(
+    x0, x1, x2, x3, g0, g1, g2, g3, w_ref, vec_ref, o_ref, c_ref, u_ref,
+    grad_ref, do_ref, dn_ref, sum_ref, hid_s, du_s, gb_s,
+):
+    up = w_ref[:, 0:96, :].reshape(D, UCOLS)
+    down = w_ref[:, 96:192, :].reshape(UCOLS, D)
+    attn = attn_rows(w_ref)
+    gain_sum = jnp.zeros((1, D), F32)
+    shift_sum = jnp.zeros((1, D), F32)
+    bias_sum = jnp.zeros((1, D), F32)
+    up_sum = jnp.zeros((1, UCOLS), F32)
+    for g, (first, second, g_first, g_second) in enumerate(((x0, x1, g0, g1), (x2, x3, g2, g3))):
+        rows = pl.ds(PAIR * g, PAIR)
+        low = jnp.concatenate([g_first[...], g_second[...]], axis=0)
+        gb_s[rows, :] = low
+        do_ref[rows, :] = mm_t(low, attn).astype(BF)
+        hidden, slope = gelu_parts(u_ref[rows, :])
+        hid_s[rows, :] = hidden.astype(BF)
+        du = (mm_t(low, down) * slope).astype(BF)
+        du_s[rows, :] = du
+        dc = mm_t(du, up)
+        scaled, _ = norm_parts(two_slots(first[0:TOK], second[0:TOK]))
+        dn_ref[rows, :] = dc * vec_ref[4:5]
+        gain_sum = gain_sum + jnp.sum(dc * scaled, axis=0, keepdims=True)
+        shift_sum = shift_sum + jnp.sum(dc, axis=0, keepdims=True)
+        bias_sum = bias_sum + jnp.sum(low.astype(F32), axis=0, keepdims=True)
+        up_sum = up_sum + jnp.sum(du.astype(F32), axis=0, keepdims=True)
+    grad_ref[:, 0:96, :] = t_mm(c_ref[...], du_s[...]).reshape(-1, 96, UCOLS).astype(BF)
+    grad_ref[:, 96:192, :] = t_mm(hid_s[...], gb_s[...]).reshape(-1, 96, D).astype(BF)
+    attn_grad = t_mm(o_ref[...], gb_s[...]).reshape(-1, 24, D)
+    grad_ref[:, 192:224, :] = jnp.concatenate(
+        [attn_grad, jnp.zeros((attn_grad.shape[0], 8, D), F32)], axis=1
+    ).astype(BF)
+    sum_ref[...] = jnp.concatenate(
+        [bias_sum, up_sum, gain_sum, shift_sum, jnp.zeros((4, D), F32)], axis=0
+    )
+
+
+def attend_back_body(
+    x0, x1, x2, x3, w_ref, vec_ref, cos_ref, sin_ref, mask_ref,
+    a_ref, q_ref, k_ref, v_ref, do_ref, dn_ref,
+    grad_ref, sum_ref, bias_ref, y0, y1, y2, y3, dp_s,
+):
+    weight = w_ref[:, 0:96, :].reshape(D, MINE)
+    gain_sum = jnp.zeros((1, D), F32)
+    shift_sum = jnp.zeros((1, D), F32)
+    bias_sum = jnp.zeros((1, MINE), F32)
+    for g, (first, second, y_first, y_second) in enumerate(((x0, x1, y0, y1), (x2, x3, y2, y3))):
+        rows = pl.ds(PAIR * g, PAIR)
+        queries, keys, values = q_ref[rows, :], k_ref[rows, :], v_ref[rows, :]
+        grad_o = do_ref[rows, :]
+        zero = jnp.zeros_like(queries)
+        dq = jnp.zeros((PAIR, HCOLS), F32)
+        dk = jnp.zeros((PAIR, HCOLS), F32)
+        dv = jnp.zeros((PAIR, HCOLS), F32)
+        for head in range(HEADS // TEAM):
+            owned = head_mask(PAIR, head)
+            scores = mm_t(jnp.where(owned, queries, zero), keys) + mask_ref[g]
+            weights = jnp.exp(scores - jnp.max(scores, axis=-1, keepdims=True))
+            weights = weights / jnp.sum(weights, axis=-1, keepdims=True)
+            dweights = mm_t(jnp.where(owned, grad_o, zero), values)
+            delta = jnp.sum(weights * dweights, axis=-1, keepdims=True)
+            dscores = (weights * (dweights - delta)).astype(BF)
+            dq = dq + jnp.where(owned, mm(dscores, keys), 0.0)
+            dk = dk + jnp.where(owned, t_mm(dscores, queries), 0.0)
+            dv = dv + jnp.where(owned, t_mm(weights.astype(BF), grad_o), 0.0)
+        both = turn(
+            jnp.concatenate([dq * 0.125, dk], axis=1), cos_ref[rows, :], -sin_ref[rows, :]
+        )
+        dproj = jnp.concatenate([both, dv], axis=1).astype(BF)
+        dp_s[rows, :] = dproj
+        bias_sum = bias_sum + jnp.sum(dproj.astype(F32), axis=0, keepdims=True)
+        da = mm_t(dproj, weight)
+        scaled, _ = norm_parts(two_slots(first[0:TOK], second[0:TOK]))
+        gain_sum = gain_sum + jnp.sum(da * scaled, axis=0, keepdims=True)
+        shift_sum = shift_sum + jnp.sum(da, axis=0, keepdims=True)
+        dn = dn_ref[rows, :] + da * vec_ref[2:3]
+        y_first[...] = dn[0:TOK].astype(y_first.dtype)
+        y_second[...] = dn[TOK:].astype(y_second.dtype)
+    grad_ref[...] = t_mm(a_ref[...], dp_s[...]).reshape(-1, 96, MINE).astype(BF)
+    sum_ref[...] = jnp.concatenate([gain_sum, shift_sum, jnp.zeros((6, D), F32)], axis=0)
+    bias_ref[...] = jnp.concatenate([bias_sum, jnp.zeros((7, MINE), F32)], axis=0)
+
+
+def norm_back_body(x_ref, g_ref, n0, n1, n2, n3, out_ref, low_ref):
+    scaled, inverse = norm_parts(x_ref[...].astype(F32))
+    dn = n0[...] + n1[...].astype(F32) + n2[...].astype(F32) + n3[...].astype(F32)
+    centered = dn - jnp.mean(dn, axis=-1, keepdims=True)
+    moment = jnp.mean(dn * scaled, axis=-1, keepdims=True)
+    result = g_ref[...].astype(F32) + inverse * (centered - scaled * moment)
+    out_ref[...] = result
+    low_ref[...] = result.astype(BF)
+
+
+def split_body(me_ref, m_ref, q_ref, o0, o1, o2, o3):
+    me = me_ref[0]
+    up = m_ref[0:96].astype(F32)
+    qkv = jnp.concatenate(
+        [q_ref[...].astype(F32), jnp.zeros((96, UCOLS - MINE), F32)], axis=1
+    )
+    for s, out in enumerate((o0, o1, o2, o3)):
+        dest = me ^ s
+        piece = jnp.concatenate([up[0:24], qkv[0:24]], axis=0)
+        for p in range(1, TEAM):
+            rows = slice(24 * p, 24 * (p + 1))
+            piece = jnp.where(dest == p, jnp.concatenate([up[rows], qkv[rows]], axis=0), piece)
+        out[...] = piece.astype(BF)
+
+
+def unpack_body(me_ref, *refs):
+    me = me_ref[0]
+    qkv_ref, up_ref = refs[-2:]
+    for depth in range(LAYERS):
+        slots = [refs[depth * TEAM + s][...].astype(F32) for s in range(TEAM)]
+        ordered = [pick(me, None, slots, p) for p in range(TEAM)]
+        blocks = FF // (96 * TEAM)
+        up_ref[depth] = jnp.concatenate(
+            [ordered[p][0:24, 96 * b : 96 * (b + 1)] for b in range(blocks) for p in range(TEAM)],
+            axis=1,
+        )
+        qkv_ref[depth] = jnp.concatenate(
+            [
+                ordered[p][24:48, HCOLS * t : HCOLS * (t + 1)]
+                for t in range(3)
+                for p in range(TEAM)
+            ],
+            axis=1,
+        )
+
+
+def team_send(piece, slot):
+    flips = [(m, m ^ slot) for m in range(TEAM)]
+    return lax.ppermute(piece, TEAM_AXES, flips)
+
+
+def local_team(
+    tokens, segment_ids, cotangent, qkv_weight, qkv_bias, attn_weight, attn_bias,
+    up_weight, up_bias, down_weight, down_bias, attn_gain, attn_shift, mlp_gain, mlp_shift,
+):
+    lines = lax.axis_size("z") * lax.axis_size("y")
+    world = lines * TEAM
+    team = lax.axis_index("z") * lax.axis_size("y") + lax.axis_index("y")
+    member = lax.axis_index("core") * 2 + lax.axis_index("x")
+    me = jnp.reshape(member, (1,)).astype(jnp.int32)
+    everywhere = LINE_AXES + TEAM_AXES
+
+    def row(vector):
+        return jnp.pad(vector, ((0, 0), (0, UCOLS - vector.shape[1])))[:, None, :]
+
+    small = jnp.concatenate(
+        [row(v) for v in (qkv_bias, up_bias, attn_gain, attn_shift, mlp_gain, mlp_shift, attn_bias, down_bias)],
+        axis=1,
+    )
+    def with_member(body, out_shape, name, operands):
+        return pl.pallas_call(
+            body,
+            out_shape=out_shape,
+            in_specs=[pl.BlockSpec(memory_space=pltpu.SMEM)]
+            + [pl.BlockSpec(memory_space=pltpu.VMEM)] * len(operands),
+            compiler_params=pltpu.CompilerParams(vmem_limit_bytes=VMEM_BYTES),
+            name=name,
+        )(me, *operands)
+
+    packed = with_member(
+        pack_body,
+        [shape((56, UCOLS), BF)] * (LAYERS * TEAM),
+        "pack_weights",
+        (qkv_weight, up_weight, small),
+    )
+
+    spread = [(i, TEAM * (i % lines) + i // lines) for i in range(world)]
+    gather_back = [(b, a) for a, b in spread]
+    attn_piece = lax.ppermute(attn_weight, everywhere, spread)
+
+    gathered = []
+    for depth in range(LAYERS):
+        mine = packed[depth * TEAM : (depth + 1) * TEAM]
+        pieces = [mine[0]] + [team_send(mine[s], s) for s in range(1, TEAM)]
+        q_part, m_part = with_member(
+            assemble_body,
+            [shape((128, MINE), BF), shape((224, D), BF)],
+            "assemble_weights",
+            (*pieces, attn_piece[depth], down_weight[depth]),
+        )
+        gathered.append(
+            (
+                lax.all_gather(q_part, LINE_AXES, axis=0),
+                lax.all_gather(m_part, LINE_AXES, axis=0),
+            )
+        )
+
+    token_slots = [tokens] + [team_send(tokens, s) for s in range(1, TEAM)]
+    segment_slots = [segment_ids] + [team_send(segment_ids, s) for s in range(1, TEAM)]
+    low_cotangent = [cotangent] + [team_send(cotangent, s) for s in range(1, TEAM)]
+    here = lax.axis_index("x")
+    rows = jnp.arange(TOK, dtype=jnp.int32)
+    places = jnp.concatenate([here * TOK + rows, (1 - here) * TOK + rows])
+    masks, cosines, sines = [], [], []
+    lane = jnp.arange(128, dtype=jnp.int32) % HEAD
+    inverse = 10000.0 ** (-(lane % (ROT // 2) * 2).astype(F32) / ROT)
+    for g in range(2):
+        ids = jnp.concatenate(segment_slots[2 * g : 2 * g + 2])
+        visible = (places[None, :] <= places[:, None]) & (ids[None, :] == ids[:, None])
+        masks.append(jnp.where(visible, 0.0, -1e30).astype(F32))
+        position = places - jnp.sum((ids[None, :] < ids[:, None]).astype(jnp.int32), axis=1)
+        phases = position.astype(F32)[:, None] * inverse[None, :]
+        cosines.append(jnp.where(lane[None, :] < ROT, jnp.cos(phases), 1.0))
+        sign = jnp.where(lane < ROT // 2, -1.0, jnp.where(lane < ROT, 1.0, 0.0))
+        sines.append(jnp.sin(phases) * sign[None, :])
+    mask = jnp.stack(masks)
+    cosine, sine = jnp.concatenate(cosines), jnp.concatenate(sines)
+
+    def vectors(depth):
+        block = gathered[depth][0][:, 96:128, :128].reshape(lines, TEAM, 8, 128)
+        wide = block[:, :, 2:8, :24].transpose(2, 0, 1, 3).reshape(6, D).astype(F32)
+        whole = jnp.concatenate([jnp.zeros((2, D), F32), wide], axis=0)
+        up_b = lax.dynamic_index_in_dim(block[:, :, 1, :96], member, 1, keepdims=False)
+        qkv_b = lax.dynamic_index_in_dim(
+            block[:, :, 0, :72].reshape(3, TEAM, HCOLS), member, 1, keepdims=False
+        )
+        return whole, up_b.reshape(1, UCOLS).astype(F32), qkv_b.reshape(1, MINE).astype(F32)
+
+    tok_all = TEAM * TOK
+    stream = tokens
+    slots = token_slots
+    kept = []
+    activations = None
+    for depth in range(LAYERS):
+        q_all, m_all = gathered[depth]
+        whole, up_b, qkv_b = vectors(depth)
+        a, q, k, v, o = call(
+            attend_body,
+            [shape((tok_all, D), BF)] + [shape((tok_all, HCOLS), BF)] * 4,
+            "attend_forward",
+            (*slots, q_all, qkv_b, whole, cosine, sine, mask),
+        )
+        c, u, y0, y1, y2, y3 = call(
+            mlp_body,
+            [shape((tok_all, D), BF), shape((tok_all, UCOLS), F32), shape((TOK, D), F32)]
+            + [shape((TOK, D), BF)] * 3,
+            "mlp_forward",
+            (*slots, m_all, up_b, whole, o),
+        )
+        kept.append((stream, slots, a, q, k, v, o, c, u, whole))
+        total = y0
+        for s, y in ((1, y1), (2, y2), (3, y3)):
+            total = total + team_send(y, s).astype(F32)
+        stream = stream.astype(F32) + total + (whole[6:7] + whole[7:8])
+        low = stream.astype(BF)
+        if depth < LAYERS - 1:
+            slots = [low] + [team_send(low, s) for s in range(1, TEAM)]
+        else:
+            activations = low
+
+    grad = cotangent
+    grad_slots = low_cotangent
+    outs, sums = [None] * LAYERS, [None] * LAYERS
+    for depth in reversed(range(LAYERS)):
+        q_all, m_all = gathered[depth]
+        stream, slots, a, q, k, v, o, c, u, whole = kept[depth]
+        m_grad, do, dn, sum_m = call(
+            mlp_back_body,
+            [
+                shape((lines, 224, D), BF),
+                shape((tok_all, HCOLS), BF),
+                shape((tok_all, D), F32),
+                shape((8, D), F32),
+            ],
+            "mlp_backward",
+            (*slots, *grad_slots, m_all, whole, o, c, u),
+            [pltpu.VMEM((tok_all, UCOLS), BF), pltpu.VMEM((tok_all, UCOLS), BF), pltpu.VMEM((tok_all, D), BF)],
+        )
+        m_sum = lax.psum_scatter(m_grad, LINE_AXES, scatter_dimension=0, tiled=False)
+        q_grad, sum_q, bias_q, n0, n1, n2, n3 = call(
+            attend_back_body,
+            [
+                shape((lines, 96, MINE), BF),
+                shape((8, D), F32),
+                shape((8, MINE), F32),
+                shape((TOK, D), F32),
+            ]
+            + [shape((TOK, D), BF)] * 3,
+            "attend_backward",
+            (*slots, q_all, whole, cosine, sine, mask, a, q, k, v, do, dn),
+            [pltpu.VMEM((tok_all, MINE), BF)],
+        )
+        q_sum = lax.psum_scatter(q_grad, LINE_AXES, scatter_dimension=0, tiled=False)
+        received = [n0] + [team_send(n, s) for s, n in ((1, n1), (2, n2), (3, n3))]
+        grad, low = call(
+            norm_back_body,
+            [shape((TOK, D), F32), shape((TOK, D), BF)],
+            "norm_backward",
+            (stream, grad, *received),
+        )
+        if depth > 0:
+            grad_slots = [low] + [team_send(low, s) for s in range(1, TEAM)]
+        mine = with_member(
+            split_body, [shape((48, UCOLS), BF)] * TEAM, "split_gradients", (m_sum, q_sum)
+        )
+        outs[depth] = (
+            [mine[0]] + [team_send(mine[s], s) for s in range(1, TEAM)],
+            m_sum[96:192].astype(F32),
+            m_sum[192:216],
+        )
+        qkv_full = lax.dynamic_update_index_in_dim(
+            jnp.zeros((3, TEAM, HCOLS), F32), bias_q[0].reshape(3, HCOLS), member, 1
+        )
+        up_full = lax.dynamic_update_index_in_dim(
+            jnp.zeros((lines, TEAM, 96), F32), sum_m[1].reshape(lines, 96), member, 1
+        )
+        bias_full = jnp.where(member == 0, sum_m[0], 0.0)
+        sums[depth] = jnp.concatenate(
+            [
+                qkv_full.reshape(world, 72),
+                up_full.reshape(world, 96),
+                *(
+                    vector.reshape(world, 24)
+                    for vector in (bias_full, sum_q[0], sum_q[1], sum_m[2], sum_m[3])
+                ),
+            ],
+            axis=1,
+        )
+    qkv_grad, up_grad = with_member(
+        unpack_body,
+        [shape((LAYERS, 24, 3 * D), F32), shape((LAYERS, 24, FF), F32)],
+        "unpack_gradients",
+        [piece for depth in range(LAYERS) for piece in outs[depth][0]],
+    )
+    down_grad = jnp.stack([outs[depth][1] for depth in range(LAYERS)])
+    attn_grad = lax.ppermute(
+        jnp.stack([outs[depth][2] for depth in range(LAYERS)]), everywhere, gather_back
+    ).astype(F32)
+    tally = jnp.stack(sums)
+    tally = tally + sum(team_send(tally, s) for s in range(1, TEAM))
+    tally = tally + lax.ppermute(tally, "y", [(0, 1), (1, 0)])
+    depth_z = lax.axis_size("z")
+    tally = tally + sum(
+        lax.ppermute(tally, "z", [(i, (i + s) % depth_z) for i in range(depth_z)])
+        for s in range(1, depth_z)
+    )
+    own = lax.dynamic_index_in_dim(tally, team * TEAM + member, 1, keepdims=False)
+    cuts = [0, 72, 168, 192, 216, 240, 264, 288]
+    qkv_b, up_b, bias, ga, sa, gm, sm = (own[:, lo:hi] for lo, hi in zip(cuts[:-1], cuts[1:]))
+    return (
+        activations, grad, qkv_grad, qkv_b, attn_grad, bias, up_grad, up_b,
+        down_grad, bias, ga, sa, gm, sm,
+    )
+
+
+def whole_mesh_solution(mesh):
     in_specs = (
         P(("dp", "cp"), None),
         P(("dp", "cp")),
@@ -479,3 +1004,18 @@
         P(None, ("dp", "cp")),
     )
     return jax.shard_map(local, mesh=mesh, in_specs=in_specs, out_specs=out_specs, check_vma=False)
+
+
+def solution(mesh):
+    teams = mesh.shape["dp"] // 2
+    if mesh.shape["cp"] != 2 or teams * TEAM * 24 != D:
+        return whole_mesh_solution(mesh)
+    split_mesh = Mesh(mesh.devices.reshape(teams // 2, 2, 2, 2), ("z", "y", "core", "x"))
+    every = ("z", "y", "core", "x")
+    row = P(every, None)
+    matrix, vector = P(None, every, None), P(None, every)
+    in_specs = (row, P(every), row) + (matrix, vector) * 4 + (vector,) * 4
+    out_specs = (row, row) + (matrix, vector) * 4 + (vector,) * 4
+    return jax.shard_map(
+        local_team, mesh=split_mesh, in_specs=in_specs, out_specs=out_specs, check_vma=False
+    )

time: 1770 us -> 554 us (0.31)
  waiting for transfers between devices: 1420 us -> 369 us
  matrix products: 106 us -> 0 us
  local copies, waits for them, and re-layouts: 117 us -> 32.6 us
  blocking collectives: 72.8 us -> 0 us
  Pallas kernels: 0 us -> 72.5 us
  starting transfers between devices: 1.77 us -> 54.1 us
    reduce_scatter x8 -> x4, waiting for transfers between devices: 998 us -> 186 us  [the longest x2 131 us: local_team(): lax.psum_scatter(m_grad, LINE_AXES, scatter_dimension=0, tiled=False)]
    all_gather x8 -> x4, waiting for transfers between devices: 360 us -> 124 us  [the longest x2 89.1 us: local_team(): lax.all_gather(m_part, LINE_AXES, axis=0)]
    dot_general x36 -> x0, matrix products: 106 us -> none  [the longest x2 17 us: local(): jnp.dot(normed_mlp, proj_up, preferred_element_type=jnp.float32)]
    pallas_call x0 -> x16, Pallas kernels: none -> 72.5 us  [the longest x10 60.7 us: call(): pl.pallas_call(body, out_shape=out_shape, scratch_shapes=list(scratch), c...]
    reshape x8 -> x4, local copies, waits for them, and re-layouts: 62.2 us -> 1.86 us  [the longest x2 1.7 us: vectors(): block = gathered[depth][0][:, 96:128, :128].reshape(lines, TEAM, 8, 128)]
    unnamed x26 -> x8, waiting for transfers between devices: 60.9 us -> 1.82 us
    ppermute x0 -> x48, waiting for transfers between devices: none -> 56.4 us  [the longest x42 50.3 us: team_send(): return lax.ppermute(piece, TEAM_AXES, flips)]
    ppermute x0 -> x48, starting transfers between devices: none -> 53.6 us  [the longest x42 38.3 us: team_send(): return lax.ppermute(piece, TEAM_AXES, flips)]
  transfers between devices with their start and end apart: 21 -> 56, of which waited for: 19 -> 25; matrix products, arithmetic and copies ran while one was open for 12% -> 5% of each run, Pallas kernels for 0% -> 9%
where the time goes in v1:
time: 554 us; the launch traced here: 551 us
  waiting for transfers between devices  369 us (67%)
  Pallas kernels  72.5 us (13%)
  starting transfers between devices  54.1 us (10%)
  local copies, waits for them, and re-layouts  32.6 us (6%)
  between operations  15 us (3%)
  other arithmetic  8.59 us (2%)
    reduce_scatter x2, waiting for transfers between devices, local_team(): lax.psum_scatter(m_grad, LINE_AXES, scatter_dimension=0, tiled=False)  131 us
    all_gather x2, waiting for transfers between devices, local_team(): lax.all_gather(m_part, LINE_AXES, axis=0)  89.1 us
    pallas_call x10, Pallas kernels, call(): pl.pallas_call(body, out_shape=out_shape, scratch_shapes=list(scratch), c...  60.7 us
    reduce_scatter x2, waiting for transfers between devices, local_team(): lax.psum_scatter(q_grad, LINE_AXES, scatter_dimension=0, tiled=False)  55 us
    ppermute x42, waiting for transfers between devices, team_send(): return lax.ppermute(piece, TEAM_AXES, flips)  50.3 us
    ppermute x42, starting transfers between devices, team_send(): return lax.ppermute(piece, TEAM_AXES, flips)  38.3 us
    all_gather x2, waiting for transfers between devices, local_team(): lax.all_gather(q_part, LINE_AXES, axis=0)  34.8 us
    pallas_call x6, Pallas kernels, with_member(): pl.pallas_call(body, out_shape=out_shape, in_specs=[pl.BlockSpec(memory_s...  11.8 us
  transfers between devices with their start and end apart: 56, of which 25 were waited for; matrix products, arithmetic and copies ran while one was open for 5% of the time, Pallas kernels for 9%

profile of v1, /device:TPU:5, one launch (start us, length us, event | category | flops | bytes accessed | tf_op | source)
XLA Modules:
  0.0 551.4 jit_solution(15781457750471508274)
XLA Ops:
  17.8 5.6 %collective-permute-start.6 = (bf16[2,24,768]{2,1,0:T(8,128)(2,1)}, bf16[2,24,768]{2,1,0:T(8,128)(2,1)S(1)}, u32[]{:S(2)}, u32[]{:S(2)}) collective-permute-start(bf16[2,24,768]{2,1,0:T(8,128)(2,1)} %param.20), channel_id=1, source_target_pairs={{0,0},{1,4},{2,8},{3,12},{4,16},{5,20},{6,24},{7,28},{8,1},{9,5},{... | collective-permute-start | bytes 221192 | tf_op jit(solution)/shard_map/ppermute | solution.py:795
  25.1 3.2 collective-permute-done.6
  44.8 6.4 %collective-permute-done.7 = s32[128]{0:T(128)S(1)} collective-permute-done((s32[128]{0:T(128)S(1)}, s32[128]{0:T(128)S(1)}, u32[]{:S(2)}, u32[]{:S(2)}) %collective-permute-start.7) | collective-permute-done | bytes 544 | tf_op jit(solution)/shard_map/ppermute | solution.py:755
  59.4 12.5 %all-gather.11.cloned.1.call-done = bf16[1024,576]{1,0:T(8,128)(2,1)} async-done(((bf16[128,576]{1,0:T(8,128)(2,1)}), bf16[1024,576]{1,0:T(8,128)(2,1)}) %all-gather.11.cloned.1.call-update) | async-done | bytes 1179664 | tf_op jit(solution)/shard_map/all_gather | solution.py:809
  76.6 5.3 attend_forward.2
  81.9 47.1 %all-gather.9.cloned.1.call-done = bf16[1792,768]{1,0:T(8,128)(2,1)} async-done(((bf16[224,768]{1,0:T(8,128)(2,1)}), bf16[1792,768]{1,0:T(8,128)(2,1)}) %all-gather.9.cloned.1.call-update) | async-done | bytes 2752528 | tf_op jit(solution)/shard_map/all_gather | solution.py:810
  129.0 5.0 mlp_forward.2
  134.0 2.9 collective-permute-start.12
  137.3 5.7 %collective-permute-done.12 = bf16[128,768]{1,0:T(8,128)(2,1)S(1)} collective-permute-done((bf16[128,768]{1,0:T(8,128)(2,1)}, bf16[128,768]{1,0:T(8,128)(2,1)S(1)}, u32[]{:S(2)}, u32[]{:S(2)}) %collective-permute-start.12) | collective-permute-done | bytes 196640 | tf_op jit(solution)/shard_map/ppermute | solution.py:755
  144.4 2.7 collective-permute-done.10
  149.9 22.3 %all-gather.15.cloned.1.call-done = bf16[1024,576]{1,0:T(8,128)(2,1)} async-done(((bf16[128,576]{1,0:T(8,128)(2,1)}), bf16[1024,576]{1,0:T(8,128)(2,1)}) %all-gather.15.cloned.1.call-update) | async-done | bytes 1179664 | tf_op jit(solution)/shard_map/all_gather | solution.py:809
  178.0 3.1 collective-permute-done.15.x3
  181.8 5.4 attend_forward.3
  187.2 42.0 %all-gather.13.cloned.1.call-done = bf16[1792,768]{1,0:T(8,128)(2,1)} async-done(((bf16[224,768]{1,0:T(8,128)(2,1)}), bf16[1792,768]{1,0:T(8,128)(2,1)}) %all-gather.13.cloned.1.call-update) | async-done | bytes 2752528 | tf_op jit(solution)/shard_map/all_gather | solution.py:810
  229.1 5.0 mlp_forward.3
  234.9 8.1 %mlp_backward.2 = (bf16[8,224,768]{2,1,0:T(8,128)(2,1)}, bf16[512,192]{1,0:T(8,128)(2,1)}, f32[512,768]{1,0:T(8,128)}, f32[8,768]{1,0:T(8,128)}) custom-call(bf16[128,768]{1,0:T(8,128)(2,1)} %copy-done.2, bf16[128,768]{1,0:T(8,128)(2,1)} %copy-done.7, bf16[128,768]{1,0:T(8,128)(2,1)} %copy-done.8, bf16[128,768]{1,0:T(8,128)(2,1)} %copy-done.9, ...), custom_call_target="tpu_custom_call" | custom-call | tf_op jit(solution)/shard_map/mlp_backward/pallas_call | solution.py:461
  243.1 9.3 %attend_backward.2 = (bf16[8,96,576]{2,1,0:T(8,128)(2,1)}, f32[8,768]{1,0:T(8,128)}, f32[8,576]{1,0:T(8,128)}, f32[128,768]{1,0:T(8,128)}, bf16[128,768]{1,0:T(8...) custom-call(bf16[128,768]{1,0:T(8,128)(2,1)} %copy-done.2, bf16[128,768]{1,0:T(8,128)(2,1)} %copy-done.7, ...), custom_call_target="tpu_custom_call" | custom-call | tf_op jit(solution)/shard_map/attend_backward/pallas_call | solution.py:461
  257.9 6.7 %collective-permute-done.27.n3 = bf16[128,768]{1,0:T(8,128)(2,1)S(1)} collective-permute-done((bf16[128,768]{1,0:T(8,128)(2,1)S(1)}, bf16[128,768]{1,0:T(8,128)(2,1)S(1)}, u32[]{:S(2)}, u32[]{:S(2)}) %collective-permute-start.27) | collective-permute-done | bytes 196640 | tf_op jit(solution)/shard_map/ppermute | solution.py:755
  265.2 2.6 norm_backward.2
  269.7 5.3 collective-permute-done.28.g1
  275.0 4.2 collective-permute-done.30.g3
  280.0 8.2 %mlp_backward.3 = (bf16[8,224,768]{2,1,0:T(8,128)(2,1)}, bf16[512,192]{1,0:T(8,128)(2,1)}, f32[512,768]{1,0:T(8,128)}, f32[8,768]{1,0:T(8,128)}) custom-call(bf16[128,768]{1,0:T(8,128)(2,1)} %x_ref.1, bf16[128,768]{1,0:T(8,128)(2,1)} %copy-done.4, bf16[128,768]{1,0:T(8,128)(2,1)} %copy-done.5, bf16[128,768]{1,0:T(8,128)(2,1)} %copy-done.6, ...), custom_call_target="tpu_custom_call" | custom-call | tf_op jit(solution)/shard_map/mlp_backward/pallas_call | solution.py:461
  289.4 9.3 %attend_backward.3 = (bf16[8,96,576]{2,1,0:T(8,128)(2,1)}, f32[8,768]{1,0:T(8,128)}, f32[8,576]{1,0:T(8,128)}, f32[128,768]{1,0:T(8,128)}, bf16[128,768]{1,0:T(8...) custom-call(bf16[128,768]{1,0:T(8,128)(2,1)} %x_ref.1, bf16[128,768]{1,0:T(8,128)(2,1)} %copy-done.4, ...), custom_call_target="tpu_custom_call" | custom-call | tf_op jit(solution)/shard_map/attend_backward/pallas_call | solution.py:461
  305.5 2.6 collective-permute-done.42
  311.6 2.9 collective-permute-done.43
  319.8 2.6 collective-permute-done.31.n1
  327.6 2.6 norm_backward.3
  330.3 61.2 %reduce-scatter.9.cloned.1.call-done = bf16[1,224,768]{2,1,0:T(8,128)(2,1)} async-done(((bf16[8,224,768]{2,1,0:T(8,128)(2,1)}), bf16[1,224,768]{2,1,0:T(8,128)(2,1)}) %reduce-scatter.9.cloned.1.call-update) | async-done | bytes 344080 | tf_op jit(solution)/shard_map/reduce_scatter | solution.py:895
  395.2 70.3 %reduce-scatter.5.cloned.1.call-done = bf16[1,224,768]{2,1,0:T(8,128)(2,1)} async-done(((bf16[8,224,768]{2,1,0:T(8,128)(2,1)}), bf16[1,224,768]{2,1,0:T(8,128)(2,1)}) %reduce-scatter.5.cloned.1.call-update) | async-done | bytes 344080 | tf_op jit(solution)/shard_map/reduce_scatter | solution.py:895
  466.3 5.0 collective-permute-start.47
  475.1 54.9 %reduce-scatter.7.cloned.1.call-done = bf16[1,96,576]{2,1,0:T(8,128)(2,1)} async-done(((bf16[8,96,576]{2,1,0:T(8,128)(2,1)}), bf16[1,96,576]{2,1,0:T(8,128)(2,1)}) %reduce-scatter.7.cloned.1.call-update) | async-done | bytes 110608 | tf_op jit(solution)/shard_map/reduce_scatter | solution.py:909
  533.9 2.9 collective-permute-start.35
  (323 shorter events, 103.6 us)
Async XLA Ops:
  7.2 64.7 %all-gather.11.cloned.1.call-start = ((), (), s32[]{:S(2)}) async-start(), calls=%async_computation.9 | async-start | bytes 1474560 | tf_op jit(solution)/shard_map/all_gather | solution.py:809
  15.5 13.5 %collective-permute-start.3 = (bf16[56,768]{1,0:T(8,128)(2,1)}, bf16[56,768]{1,0:T(8,128)(2,1)S(1)}, u32[]{:S(2)}, u32[]{:S(2)}) collective-permute-start(bf16[56,768]{1,0:T(8,128)(2,1)} %get-tuple-element.84), channel_id=1, source_target_pairs={{0,1},{1,0},{2,3},{3,2},{4,5},{5,4},{6,7},{7,6},{8,9},{9,8},{10,11... | collective-permute-start | bytes 258056 | tf_op jit(solution)/shard_map/ppermute | solution.py:755
  16.7 12.2 %collective-permute-start.4 = (bf16[56,768]{1,0:T(8,128)(2,1)}, bf16[56,768]{1,0:T(8,128)(2,1)S(1)}, u32[]{:S(2)}, u32[]{:S(2)}) collective-permute-start(bf16[56,768]{1,0:T(8,128)(2,1)} %get-tuple-element.85), channel_id=1, source_target_pairs={{0,2},{1,3},{2,0},{3,1},{4,6},{5,7},{6,4},{7,5},{8,10},{9,11},{10,... | collective-permute-start | bytes 258056 | tf_op jit(solution)/shard_map/ppermute | solution.py:755
  17.7 11.3 %collective-permute-start.5 = (bf16[56,768]{1,0:T(8,128)(2,1)}, bf16[56,768]{1,0:T(8,128)(2,1)S(1)}, u32[]{:S(2)}, u32[]{:S(2)}) collective-permute-start(bf16[56,768]{1,0:T(8,128)(2,1)} %get-tuple-element.86), channel_id=1, source_target_pairs={{0,3},{1,2},{2,1},{3,0},{4,7},{5,6},{6,5},{7,4},{8,11},{9,10},{10,... | collective-permute-start | bytes 258056 | tf_op jit(solution)/shard_map/ppermute | solution.py:755
  17.8 10.5 %collective-permute-start.6 = (bf16[2,24,768]{2,1,0:T(8,128)(2,1)}, bf16[2,24,768]{2,1,0:T(8,128)(2,1)S(1)}, u32[]{:S(2)}, u32[]{:S(2)}) collective-permute-start(bf16[2,24,768]{2,1,0:T(8,128)(2,1)} %param.20), channel_id=1, source_target_pairs={{0,0},{1,4},{2,8},{3,12},{4,16},{5,20},{6,24},{7,28},{8,1},{9,5},{... | collective-permute-start | bytes 221192 | tf_op jit(solution)/shard_map/ppermute | solution.py:795
  31.6 97.4 %all-gather.9.cloned.1.call-start = ((), (), s32[]{:S(2)}) async-start(), calls=%async_computation.8 | async-start | bytes 3096576 | tf_op jit(solution)/shard_map/all_gather | solution.py:810
  32.4 139.7 %all-gather.15.cloned.1.call-start = ((), (), s32[]{:S(2)}) async-start(), calls=%async_computation.11 | async-start | bytes 1474560 | tf_op jit(solution)/shard_map/all_gather | solution.py:809
  40.4 188.8 %all-gather.13.cloned.1.call-start = ((), (), s32[]{:S(2)}) async-start(), calls=%async_computation.10 | async-start | bytes 3096576 | tf_op jit(solution)/shard_map/all_gather | solution.py:810
  40.9 289.3 %reduce-scatter.11.cloned.1.call-start = ((), (), s32[]{:S(2)}) async-start(), calls=%async_computation.7 | async-start | bytes 1105920 | tf_op jit(solution)/shard_map/reduce_scatter | solution.py:909
  41.0 34.1 %collective-permute-start = (bf16[128,768]{1,0:T(8,128)(2,1)S(1)}, bf16[128,768]{1,0:T(8,128)(2,1)S(1)}, u32[]{:S(2)}, u32[]{:S(2)}) collective-permute-start(bf16[128,768]{1,0:T(8,128)(2,1)S(1)} %copy-done), channel_id=1, source_target_pairs={{0,1},{1,0},{2,3},{3,2},{4,5},{5,4},{6,7},{7,6},{8,9},{9,8},{10,11... | collective-permute-start | bytes 589832 | tf_op jit(solution)/shard_map/ppermute | solution.py:755
  42.0 33.2 %collective-permute-start.1 = (bf16[128,768]{1,0:T(8,128)(2,1)S(1)}, bf16[128,768]{1,0:T(8,128)(2,1)S(1)}, u32[]{:S(2)}, u32[]{:S(2)}) collective-permute-start(bf16[128,768]{1,0:T(8,128)(2,1)S(1)} %copy-done), channel_id=1, source_target_pairs={{0,2},{1,3},{2,0},{3,1},{4,6},{5,7},{6,4},{7,5},{8,10},{9,11},{10,... | collective-permute-start | bytes 589832 | tf_op jit(solution)/shard_map/ppermute | solution.py:755
  42.6 32.5 %collective-permute-start.2 = (bf16[128,768]{1,0:T(8,128)(2,1)S(1)}, bf16[128,768]{1,0:T(8,128)(2,1)S(1)}, u32[]{:S(2)}, u32[]{:S(2)}) collective-permute-start(bf16[128,768]{1,0:T(8,128)(2,1)S(1)} %copy-done), channel_id=1, source_target_pairs={{0,3},{1,2},{2,1},{3,0},{4,7},{5,6},{6,5},{7,4},{8,11},{9,10},{10,... | collective-permute-start | bytes 589832 | tf_op jit(solution)/shard_map/ppermute | solution.py:755
  53.4 180.7 %collective-permute-start.22 = (bf16[128,768]{1,0:T(8,128)(2,1)S(1)}, bf16[128,768]{1,0:T(8,128)(2,1)S(1)}, u32[]{:S(2)}, u32[]{:S(2)}) collective-permute-start(bf16[128,768]{1,0:T(8,128)(2,1)S(1)} %copy-done.10), channel_id=1, source_target_pairs={{0,1},{1,0},{2,3},{3,2},{4,5},{5,4},{6,7},{7,6},{8,9},{9,8},{10,11... | collective-permute-start | bytes 589832 | tf_op jit(solution)/shard_map/ppermute | solution.py:755
  54.6 179.5 %collective-permute-start.23 = (bf16[128,768]{1,0:T(8,128)(2,1)S(1)}, bf16[128,768]{1,0:T(8,128)(2,1)S(1)}, u32[]{:S(2)}, u32[]{:S(2)}) collective-permute-start(bf16[128,768]{1,0:T(8,128)(2,1)S(1)} %copy-done.10), channel_id=1, source_target_pairs={{0,2},{1,3},{2,0},{3,1},{4,6},{5,7},{6,4},{7,5},{8,10},{9,11},{10,... | collective-permute-start | bytes 589832 | tf_op jit(solution)/shard_map/ppermute | solution.py:755
  143.0 91.1 %collective-permute-start.24 = (bf16[128,768]{1,0:T(8,128)(2,1)S(1)}, bf16[128,768]{1,0:T(8,128)(2,1)S(1)}, u32[]{:S(2)}, u32[]{:S(2)}) collective-permute-start(bf16[128,768]{1,0:T(8,128)(2,1)S(1)} %copy-done.10), channel_id=1, source_target_pairs={{0,3},{1,2},{2,1},{3,0},{4,7},{5,6},{6,5},{7,4},{8,11},{9,10},{10,... | collective-permute-start | bytes 589832 | tf_op jit(solution)/shard_map/ppermute | solution.py:755
  149.0 25.5 %collective-permute-start.13 = (bf16[128,768]{1,0:T(8,128)(2,1)S(1)}, bf16[128,768]{1,0:T(8,128)(2,1)S(1)}, u32[]{:S(2)}, u32[]{:S(2)}) collective-permute-start(bf16[128,768]{1,0:T(8,128)(2,1)S(1)} %get-tuple-element.164.x0), channel_id=1, source_target_pairs={{0,1},{1,0},{2,3},{3,2},{4,5},{5,4},{6,7},{7,6},{8,9},{9,8},{10,11... | collective-permute-start | bytes 589832 | tf_op jit(solution)/shard_map/ppermute | solution.py:755
  252.4 139.1 %reduce-scatter.9.cloned.1.call-start = ((), (), s32[]{:S(2)}) async-start(), calls=%async_computation.6 | async-start | bytes 3096576 | tf_op jit(solution)/shard_map/reduce_scatter | solution.py:895
  253.0 212.5 %reduce-scatter.5.cloned.1.call-start = ((), (), s32[]{:S(2)}) async-start(), calls=%async_computation.4 | async-start | bytes 3096576 | tf_op jit(solution)/shard_map/reduce_scatter | solution.py:895
  269.0 10.3 %collective-permute-start.30 = (bf16[128,768]{1,0:T(8,128)(2,1)}, bf16[128,768]{1,0:T(8,128)(2,1)S(1)}, u32[]{:S(2)}, u32[]{:S(2)}) collective-permute-start(bf16[128,768]{1,0:T(8,128)(2,1)} %get-tuple-element.122.g0), channel_id=1, source_target_pairs={{0,3},{1,2},{2,1},{3,0},{4,7},{5,6},{6,5},{7,4},{8,11},{9,10},{10,... | collective-permute-start | bytes 589832 | tf_op jit(solution)/shard_map/ppermute | solution.py:755
  288.1 241.9 %reduce-scatter.7.cloned.1.call-start = ((), (), s32[]{:S(2)}) async-start(), calls=%async_computation.5 | async-start | bytes 1105920 | tf_op jit(solution)/shard_map/reduce_scatter | solution.py:909
  305.1 10.9 %collective-permute-start.21 = (bf16[128,768]{1,0:T(8,128)(2,1)S(1)}, bf16[128,768]{1,0:T(8,128)(2,1)S(1)}, u32[]{:S(2)}, u32[]{:S(2)}) collective-permute-start(bf16[128,768]{1,0:T(8,128)(2,1)S(1)} %copy-done.41), channel_id=1, source_target_pairs={{0,3},{1,2},{2,1},{3,0},{4,7},{5,6},{6,5},{7,4},{8,11},{9,10},{10,... | collective-permute-start | bytes 589832 | tf_op jit(solution)/shard_map/ppermute | solution.py:755
  305.4 12.1 %collective-permute-start.20 = (bf16[128,768]{1,0:T(8,128)(2,1)S(1)}, bf16[128,768]{1,0:T(8,128)(2,1)S(1)}, u32[]{:S(2)}, u32[]{:S(2)}) collective-permute-start(bf16[128,768]{1,0:T(8,128)(2,1)S(1)} %copy-done.40), channel_id=1, source_target_pairs={{0,2},{1,3},{2,0},{3,1},{4,6},{5,7},{6,4},{7,5},{8,10},{9,11},{10,... | collective-permute-start | bytes 589832 | tf_op jit(solution)/shard_map/ppermute | solution.py:755
  308.2 11.6 %collective-permute-start.19 = (bf16[128,768]{1,0:T(8,128)(2,1)S(1)}, bf16[128,768]{1,0:T(8,128)(2,1)S(1)}, u32[]{:S(2)}, u32[]{:S(2)}) collective-permute-start(bf16[128,768]{1,0:T(8,128)(2,1)S(1)} %copy-done.39), channel_id=1, source_target_pairs={{0,1},{1,0},{2,3},{3,2},{4,5},{5,4},{6,7},{7,6},{8,9},{9,8},{10,11... | collective-permute-start | bytes 589832 | tf_op jit(solution)/shard_map/ppermute | solution.py:755
  309.8 12.6 %collective-permute-start.31 = (bf16[128,768]{1,0:T(8,128)(2,1)S(1)}, bf16[128,768]{1,0:T(8,128)(2,1)S(1)}, u32[]{:S(2)}, u32[]{:S(2)}) collective-permute-start(bf16[128,768]{1,0:T(8,128)(2,1)S(1)} %copy-done.44), channel_id=1, source_target_pairs={{0,1},{1,0},{2,3},{3,2},{4,5},{5,4},{6,7},{7,6},{8,9},{9,8},{10,11... | collective-permute-start | bytes 589832 | tf_op jit(solution)/shard_map/ppermute | solution.py:755
  314.5 10.2 %collective-permute-start.32 = (bf16[128,768]{1,0:T(8,128)(2,1)S(1)}, bf16[128,768]{1,0:T(8,128)(2,1)S(1)}, u32[]{:S(2)}, u32[]{:S(2)}) collective-permute-start(bf16[128,768]{1,0:T(8,128)(2,1)S(1)} %copy-done.43), channel_id=1, source_target_pairs={{0,2},{1,3},{2,0},{3,1},{4,6},{5,7},{6,4},{7,5},{8,10},{9,11},{10,... | collective-permute-start | bytes 589832 | tf_op jit(solution)/shard_map/ppermute | solution.py:755
  316.0 11.0 %collective-permute-start.33 = (bf16[128,768]{1,0:T(8,128)(2,1)S(1)}, bf16[128,768]{1,0:T(8,128)(2,1)S(1)}, u32[]{:S(2)}, u32[]{:S(2)}) collective-permute-start(bf16[128,768]{1,0:T(8,128)(2,1)S(1)} %copy-done.42), channel_id=1, source_target_pairs={{0,3},{1,2},{2,1},{3,0},{4,7},{5,6},{6,5},{7,4},{8,11},{9,10},{10,... | collective-permute-start | bytes 589832 | tf_op jit(solution)/shard_map/ppermute | solution.py:755
  317.4 12.8 %collective-permute-start.46 = (f32[2,32,288]{2,0,1:T(2,128)S(1)}, f32[2,32,288]{2,0,1:T(2,128)S(1)}, u32[]{:S(2)}, u32[]{:S(2)}) collective-permute-start(f32[2,32,288]{2,0,1:T(2,128)S(1)} %add.209), channel_id=1, source_target_pairs={{0,24},{8,0},{16,8},{24,16},{1,25},{9,1},{17,9},{25,17},{2,26},{10... | collective-permute-start | bytes 221192 | tf_op jit(solution)/shard_map/ppermute | solution.py:960
  319.8 10.4 %collective-permute-start.45 = (f32[2,32,288]{2,0,1:T(2,128)S(1)}, f32[2,32,288]{2,0,1:T(2,128)S(1)}, u32[]{:S(2)}, u32[]{:S(2)}) collective-permute-start(f32[2,32,288]{2,0,1:T(2,128)S(1)} %add.209), channel_id=1, source_target_pairs={{0,16},{8,24},{16,0},{24,8},{1,17},{9,25},{17,1},{25,9},{2,18},{10... | collective-permute-start | bytes 221192 | tf_op jit(solution)/shard_map/ppermute | solution.py:960
  393.3 140.6 %collective-permute-start.37 = (bf16[48,768]{1,0:T(8,128)(2,1)}, bf16[48,768]{1,0:T(8,128)(2,1)S(1)}, u32[]{:S(2)}, u32[]{:S(2)}) collective-permute-start(bf16[48,768]{1,0:T(8,128)(2,1)} %get-tuple-element.141), channel_id=1, source_target_pairs={{0,1},{1,0},{2,3},{3,2},{4,5},{5,4},{6,7},{7,6},{8,9},{9,8},{10,11... | collective-permute-start | bytes 221192 | tf_op jit(solution)/shard_map/ppermute | solution.py:755
  466.3 70.6 %collective-permute-start.47 = (bf16[2,24,768]{2,1,0:T(8,128)(2,1)S(1)}, bf16[2,24,768]{2,1,0:T(8,128)(2,1)S(1)}, u32[]{:S(2)}, u32[]{:S(2)}) collective-permute-start(bf16[2,24,768]{2,1,0:T(8,128)(2,1)S(1)} %pad_maximum_fusion.4), channel_id=1, source_target_pairs={{0,0},{4,1},{8,2},{12,3},{16,4},{20,5},{24,6},{28,7},{1,8},{5,9},{... | collective-permute-start | bytes 221192 | tf_op jit(solution)/shard_map/ppermute | solution.py:952
  473.1 65.5 %collective-permute-start.38 = (bf16[48,768]{1,0:T(8,128)(2,1)}, bf16[48,768]{1,0:T(8,128)(2,1)S(1)}, u32[]{:S(2)}, u32[]{:S(2)}) collective-permute-start(bf16[48,768]{1,0:T(8,128)(2,1)} %get-tuple-element.142), channel_id=1, source_target_pairs={{0,2},{1,3},{2,0},{3,1},{4,6},{5,7},{6,4},{7,5},{8,10},{9,11},{10,... | collective-permute-start | bytes 221192 | tf_op jit(solution)/shard_map/ppermute | solution.py:755
  473.1 65.5 %collective-permute-start.39 = (bf16[48,768]{1,0:T(8,128)(2,1)}, bf16[48,768]{1,0:T(8,128)(2,1)S(1)}, u32[]{:S(2)}, u32[]{:S(2)}) collective-permute-start(bf16[48,768]{1,0:T(8,128)(2,1)} %get-tuple-element.143), channel_id=1, source_target_pairs={{0,3},{1,2},{2,1},{3,0},{4,7},{5,6},{6,5},{7,4},{8,11},{9,10},{10,... | collective-permute-start | bytes 221192 | tf_op jit(solution)/shard_map/ppermute | solution.py:755
  (76 other events, 620.6 us)
Sparse Core Ops, SparseCore 0:
  31.7 40.1 all-gather.10
  74.7 54.2 all-gather.8
  131.2 40.8 all-gather.14
  174.7 54.3 all-gather.12
  252.5 61.9 reduce-scatter.10
  318.3 73.1 reduce-scatter.8
  395.4 69.9 reduce-scatter.4
  469.2 60.8 reduce-scatter.6
